TPU v7x, 128 devices: a whole 4x4x4 slice. The times are simulated.
128 devices in a mesh: dp: 16 (over z_hi, x, core), tensor: 8 (over y, z_lo).
Axes of the slice: x: 4, y: 4, z: 4 (z_hi: 2, z_lo: 2; z = z_hi * 2 + z_lo), core: 2. Of those that a mesh axis runs over, the one named last changes fastest.
Arguments:
- tokens: bfloat16 [16384, 4096], P(('dp', 'tensor')), may hold values from -6 to 6
- in_weight: bfloat16 [4096, 20608], P(('dp', 'tensor')), may hold values from -0.09375 to 0.09375
- group_order: int32 [8], replicated, may hold values from 0 to 7, each once
- head_order: int32 [8, 16], replicated, may hold values from 0 to 15, each once within a row
- conv_x: float32 [4, 8192], P(None, 'tensor'), may hold values from -3 to 3
- conv_bc: float32 [4, 4096], P(None, 'tensor'), may hold values from -3 to 3
- dt_bias: float32 [128], P('tensor'), may hold values from -3 to 1
Outputs:
- gated: bfloat16 [16384, 8192], P('dp', 'tensor')
- bc_out: bfloat16 [16384, 4096], P('dp', 'tensor')
- dt_out: float32 [16384, 128], P('dp', 'tensor')
Inputs may be any that keep to these rules, and one draw needn't show every extreme that they name: `group_order`: each value once. `head_order`: each row holds each value once.
All inputs are finite; a program needn't handle non-finite values.
Results may differ from a plain program's by a relative error of at most 0.0062.
Values may be sent and summed in bfloat16 or wider, within the bound.
A program may use at most 128 MiB of HBM per device.

v0:
```python
import jax
import jax.numpy as jnp
from jax import lax
from jax.sharding import PartitionSpec as P

P_SIZE = 64
HPG = 16
N = 256
KW = 4


def from_behind(value, axis, steps):
    count = lax.axis_size(axis)
    leading, last = (max(0, -steps), min(count, count - steps))
    return lax.ppermute(value, axis, [(source, source + steps) for source in range(leading, last)])


def permute_block(column_block, head_perm):
    row_count = column_block.shape[0]
    head_cols = HPG * P_SIZE
    gate_part = jnp.take(
        column_block[:, :head_cols].reshape(row_count, HPG, P_SIZE), head_perm, axis=1
    ).reshape(row_count, head_cols)
    value_part = jnp.take(
        column_block[:, head_cols : 2 * head_cols].reshape(row_count, HPG, P_SIZE),
        head_perm,
        axis=1,
    ).reshape(row_count, head_cols)
    state_part = column_block[:, 2 * head_cols : 2 * head_cols + 2 * N]
    step_part = jnp.take(column_block[:, 2 * head_cols + 2 * N :], head_perm, axis=1)
    return jnp.concatenate([gate_part, value_part, state_part, step_part], axis=1)


def on_device(tokens, in_weight, group_order, head_order, conv_x, conv_bc, dt_bias):
    slot_index = lax.axis_index("tensor")
    head_cols = HPG * P_SIZE
    group_width = 2 * HPG * P_SIZE + 2 * N + HPG
    trainer_block = lax.all_gather(in_weight, "tensor", axis=0, tiled=True)
    group_pick = group_order[slot_index]
    column_block = lax.dynamic_slice_in_dim(trainer_block, group_pick * group_width, group_width, 1)
    column_block = permute_block(column_block, head_order[slot_index])
    group_tokens = lax.all_gather(tokens, "tensor", axis=0, tiled=True)
    token_count = group_tokens.shape[0]
    summed = jnp.dot(
        group_tokens,
        lax.all_gather(column_block, "dp", axis=0, tiled=True),
        preferred_element_type=jnp.float32,
    )
    projected = summed.astype(jnp.bfloat16)
    mixing = projected[:, head_cols : 2 * head_cols + 2 * N]
    rim_rows = from_behind(mixing[token_count - (KW - 1) :], "dp", 1)
    gate_raw = projected[:, :head_cols]
    step_raw = projected[:, 2 * head_cols + 2 * N :]
    kernel = jnp.concatenate([conv_x, conv_bc], axis=1)
    extended = jnp.concatenate([rim_rows, mixing], axis=0)
    running = kernel[0] * extended[0:token_count].astype(jnp.float32)
    for position in range(1, KW):
        running = running + kernel[position] * extended[position : position + token_count].astype(
            jnp.float32
        )
    gated = (
        jax.nn.silu(running[:, :head_cols]) * jax.nn.silu(gate_raw.astype(jnp.float32))
    ).astype(jnp.bfloat16)
    states = jax.nn.silu(running[:, head_cols:]).astype(jnp.bfloat16)
    steps_out = jax.nn.softplus(step_raw.astype(jnp.float32) + dt_bias)
    return (gated, states, steps_out)


def solution(mesh):
    return jax.shard_map(
        on_device,
        mesh=mesh,
        in_specs=(
            P(("dp", "tensor"), None),
            P(("dp", "tensor"), None),
            P(),
            P(),
            P(None, "tensor"),
            P(None, "tensor"),
            P("tensor"),
        ),
        out_specs=(P("dp", "tensor"), P("dp", "tensor"), P("dp", "tensor")),
        check_vma=False,
    )
```

profile of v0, /device:TPU:0, one launch (start us, length us, event | category | flops | bytes accessed | tf_op | source)
XLA Modules:
  0.0 596.6 jit_solution(617189230598962242)
XLA Ops:
  7.2 0.0 all-gather.4.cloned.1.call-start
  7.2 0.7 all-gather.4.cloned.1.call-update
  7.9 0.0 all-gather.8.cloned.1.call-start
  7.9 0.7 all-gather.8.cloned.1.call-update
  8.6 0.0 all-gather.6.cloned.1.call-start
  8.7 1.2 dynamic_slice.9
  10.6 0.7 fusion.8
  11.3 0.7 compare_and_fusion
  12.0 209.1 %all-gather.4.cloned.1.call-done = bf16[256,20608]{1,0:T(8,128)(2,1)} async-done(((bf16[32,20608]{1,0:T(8,128)(2,1)}), bf16[256,20608]{1,0:T(8,128)(2,1)}) %all-gather.4.cloned.1.call-update) | async-done | bytes 10551312 | tf_op jit(solution)/shard_map/all_gather | solution.py:38
  221.1 1.9 constant_dynamic-slice_fusion.2
  223.0 0.2 copy.17
  223.2 0.2 copy.18
  223.4 0.6 gather_fusion.1
  224.0 0.6 gather_fusion.2
  224.5 0.0 copy-start
  224.6 0.0 copy-start.1
  224.6 0.9 constant_dynamic-slice_fusion.4
  225.5 0.1 copy.20
  225.6 1.1 constant_dynamic-slice_fusion
  226.7 0.1 copy.19
  226.9 0.6 gather_fusion
  227.4 0.1 select_bitcast_fusion
  227.5 0.2 broadcast_select_fusion.1
  227.7 1.1 pad_maximum_fusion.1
  228.8 0.0 all-gather.6.cloned.1.call-update
  228.9 0.0 copy-done
  228.9 0.0 copy-done.1
  228.9 0.1 slice_reduce_fusion.3
  229.0 0.0 copy-start.2
  229.0 163.6 %all-gather.8.cloned.1.call-done = bf16[1024,4096]{1,0:T(8,128)(2,1)} async-done(((bf16[128,4096]{1,0:T(8,128)(2,1)}), bf16[1024,4096]{1,0:T(8,128)(2,1)}) %all-gather.8.cloned.1.call-update) | async-done | bytes 8388624 | tf_op jit(solution)/shard_map/all_gather | solution.py:42
  392.6 154.0 %all-gather.6.cloned.1.call-done = bf16[4096,2576]{0,1:T(8,128)(2,1)} async-done(((bf16[256,2576]{0,1:T(8,128)(2,1)}), bf16[4096,2576]{0,1:T(8,128)(2,1)}) %all-gather.6.cloned.1.call-update) | async-done | bytes 21102608 | tf_op jit(solution)/shard_map/all_gather | solution.py:46
  546.6 27.7 %fusion = bf16[1024,2576]{0,1:T(8,128)(2,1)S(1)} fusion(bf16[4096,2576]{0,1:T(8,128)(2,1)} %all-gather.6.cloned.1.call-done, bf16[1024,4096]{1,0:T(8,128)(2,1)} %all-gather.8.cloned.1.call-done), kind=kOutput, calls=%fused_computation.7 | convolution fusion | flops 21611692032 | bytes 34766848 | tf_op jit(solution)/shard_map/dot_general | solution.py:44
  574.3 0.2 slice.76
  574.5 2.2 collective-permute-start
  576.7 0.0 copy-done.2
  576.7 0.7 compare_select_fusion
  577.5 0.3 slice.77
  577.8 0.2 collective-permute-done
  578.0 5.2 multiply_add_fusion
  583.3 2.4 fusion.5
  585.7 0.6 multiply_convert_fusion
  586.2 2.6 copy.14
  588.8 1.3 copy.15
  (4 shorter events, 0.0 us)
Async XLA Ops:
  7.2 213.9 %all-gather.4.cloned.1.call-start = ((), (), s32[]{:S(2)}) async-start(), calls=%async_computation | async-start | bytes 11870208 | tf_op jit(solution)/shard_map/all_gather | solution.py:38
  7.9 384.7 %all-gather.8.cloned.1.call-start = ((), (), s32[]{:S(2)}) async-start(), calls=%async_computation.2 | async-start | bytes 9437184 | tf_op jit(solution)/shard_map/all_gather | solution.py:42
  8.6 538.0 %all-gather.6.cloned.1.call-start = ((), (), s32[]{:S(2)}) async-start(), calls=%async_computation.1 | async-start | bytes 22421504 | tf_op jit(solution)/shard_map/all_gather | solution.py:46
  224.5 4.3 copy-start
  224.6 4.3 copy-start.1
  229.0 347.8 %copy-start.2 = (f32[16]{0:T(128)S(1)}, f32[16]{0:T(128)}, u32[]{:S(2)}) copy-start(f32[16]{0:T(128)} %param.15) | copy-start | bytes 196
  574.5 3.5 collective-permute-start
Sparse Core Ops, SparseCore 0:
  9.6 211.4 all-gather.3
  222.7 169.8 all-gather.7
  395.4 151.1 all-gather.5
where the time goes:
time: 603 us; the launch traced here: 597 us
  waiting for transfers between devices  528 us (88%)
  matrix products  27.7 us (5%)
  between operations  14.6 us (2%)
  local copies, waits for them, and re-layouts  12 us (2%)
  other arithmetic  11.7 us (2%)
    all_gather x1, waiting for transfers between devices, on_device(): trainer_block = lax.all_gather(in_weight, 'tensor', axis=0, tiled=True)  209 us
    all_gather x1, waiting for transfers between devices, on_device(): group_tokens = lax.all_gather(tokens, 'tensor', axis=0, tiled=True)  164 us
    all_gather x1, waiting for transfers between devices, on_device(): lax.all_gather(column_block, 'dp', axis=0, tiled=True)  154 us
    dot_general x1, matrix products, on_device(): jnp.dot(group_tokens, lax.all_gather(column_block, 'dp', axis=0, tiled=Tr...  27.7 us
  transfers between devices with their start and end apart: 4, of which 4 were waited for; matrix products, arithmetic and copies ran while one was open for 2% of the time, Pallas kernels for 0%

commit v1 on v0

v1 whole, which is shorter than its diff:
```python
import functools

import jax
import jax.numpy as jnp
from jax import lax
from jax.experimental import pallas as pl
from jax.experimental.pallas import tpu as pltpu
from jax.sharding import PartitionSpec as P

MESH = pl.DeviceIdType.MESH
HEAD = 64
HPG = 16
N = 256
GW = 2 * HPG * HEAD + 2 * N + HPG
D = 4096
ROWS = 1024
TOK = 128
KB = 256
KR = 32
GRP = 256
HALO = 16
CW = 512
ORDER = ("dt", 0, 1, 2, 3, 4)


def arrange(group_order, head_order, w_own, stage, stage_dt, lined):
    lane = lax.broadcasted_iota(jnp.int32, (KR, 128), 1)

    def line_up(slot):
        group = group_order[slot]
        for part in range(4):
            start = pl.multiple_of((20 * group + 5 * part) * 128, 128)
            wide = pltpu.roll(w_own[:, pl.ds(start, 768)].astype(jnp.float32), (768 - 16 * group) % 768, 1)
            lined[:, 640 * part : 640 * part + 640] = wide[:, :640]
        start = pl.multiple_of((20 * group + 20) * 128, 128)
        tile = pltpu.roll(w_own[:, pl.ds(start, 128)].astype(jnp.float32), (128 - 16 * group) % 128, 1)
        lined[:, 2560:2688] = jnp.where(lane < HPG, tile, 0.0)

    def head_tile(slot, base, first):
        parts = []
        for half in range(2):
            picked = head_order[slot, first + half]
            start = pl.multiple_of(base + 128 * (picked >> 1), 128)
            tile = lined[:, pl.ds(start, 128)]
            parts.append(jnp.where((picked & 1) == half, tile, pltpu.roll(tile, HEAD, 1)))
        return jnp.where(lane < HEAD, parts[0], parts[1]).astype(jnp.bfloat16)

    def make(chunk, slot, store):
        if chunk == "dt":
            source = jnp.full((128, 128), 128, jnp.int32)
            across = lax.broadcasted_iota(jnp.int32, (128, 128), 1)
            for j in range(HPG):
                source = jnp.where(across == j, head_order[slot, j], source)
            down = lax.broadcasted_iota(jnp.int32, (128, 128), 0)
            pick = (down == source).astype(jnp.float32).astype(jnp.bfloat16)
            tile = lined[:, 2560:2688].astype(jnp.bfloat16)
            store(0, jnp.dot(tile, pick, preferred_element_type=jnp.float32).astype(jnp.bfloat16))
        elif chunk == 4:
            for tile in range(4):
                store(tile, lined[:, 2048 + 128 * tile : 2176 + 128 * tile].astype(jnp.bfloat16))
        else:
            for part in range(2):
                for pair in range(2):
                    store(2 * part + pair, head_tile(slot, 1024 * part, 4 * chunk + 2 * pair))

    def body(slot, carry):
        line_up(slot)

        def store_dt(tile, value):
            stage_dt[slot] = value

        make("dt", slot, store_dt)
        for chunk in range(5):

            def store(tile, value, chunk=chunk):
                stage[chunk, slot, :, 128 * tile : 128 * tile + 128] = value

            make(chunk, slot, store)
        return carry

    lax.fori_loop(0, 8, body, 0)


def kernel(
    tokens, stage, stage_dt, conv_x, conv_bc, dt_bias,
    gated, states, steps,
    panel, panel_dt, tok, proj, gated_v, states_v,
    a2a_sem, z_sem, ring_sem, sib_sem, send_sem, t_sem, t_send, h_sem, h_send, own_sem, out_sem,
):
    dp, ten = lax.axis_index("dp"), lax.axis_index("tensor")
    core, x, zh = dp % 2, (dp // 2) % 4, dp // 8
    y, zl = ten // 2, ten % 2

    def dp_of(zh_, x_, core_):
        return (zh_ * 4 + x_) * 2 + core_

    left, right, opposite = (x + 3) % 4, (x + 1) % 4, (x + 2) % 4
    up, down, far = (y + 1) % 4, (y + 3) % 4, (y + 2) % 4
    at_right = (dp_of(zh, right, core), ten)
    at_left = (dp_of(zh, left, core), ten)
    at_zh = (dp_of(1 - zh, x, core), ten)
    at_sib = (dp_of(zh, x, 1 - core), ten)
    at_up = (dp, up * 2 + zl)
    at_down = (dp, down * 2 + zl)
    at_zl = (dp, y * 2 + 1 - zl)
    after, before = ((dp + 1) % 16, ten), ((dp + 15) % 16, ten)

    load_t = pltpu.make_async_copy(tokens, tok.at[pl.ds(HALO + ten * TOK, TOK)], own_sem)
    load_t.start()

    barrier = pltpu.get_barrier_semaphore()
    for step in range(1, 8):
        pl.semaphore_signal(barrier, inc=1, device_id=(dp, (ten + step) % 8), device_id_type=MESH)
    for peer in (at_right, at_left, at_zh, at_sib, after, before):
        pl.semaphore_signal(barrier, inc=1, device_id=peer, device_id_type=MESH)

    def remote(src, dst, send, recv, peer):
        return pltpu.make_async_remote_copy(
            src_ref=src, dst_ref=dst, send_sem=send, recv_sem=recv, device_id=peer, device_id_type=MESH
        )

    def tok_rows(y_, zl_):
        return tok.at[pl.ds(HALO + (y_ * 2 + zl_) * TOK, TOK)]

    def tok_send(src, dst, sem, peer):
        remote(src, dst, t_send, t_sem.at[sem], peer).start()

    def tok_wait(sem, y_, zl_):
        ref = tok_rows(y_, zl_)
        pltpu.make_async_copy(ref, ref, t_sem.at[sem]).wait()

    ZL, L0, R0, L1, R1, O0, O1 = range(7)

    def tok_pair():
        tok_wait(ZL, y, 1 - zl)
        ref = tok_rows(y, 1 - zl)
        tok_send(ref, ref, L1, at_up)
        tok_send(ref, ref, R1, at_down)

    def tok_near():
        tok_wait(L0, down, zl)
        ref = tok_rows(down, zl)
        tok_send(ref, ref, O0, at_up)
        tok_wait(R0, up, zl)

    def tok_next():
        tok_wait(R1, up, 1 - zl)
        ref = tok_rows(up, 1 - zl)
        tok_send(ref, ref, O1, at_down)
        tok_wait(L1, down, 1 - zl)

    def tok_far():
        tok_wait(O0, far, zl)
        tok_wait(O1, far, 1 - zl)

    tail = tok.at[pl.ds(ROWS, HALO)]
    head = tok.at[pl.ds(0, HALO)]

    def halo_send(where):
        @pl.when(jnp.logical_and(where, dp < 15))
        def _():
            remote(tail, head, h_send, h_sem, after).start()

    def halo_wait(where):
        @pl.when(jnp.logical_and(where, dp > 0))
        def _():
            pltpu.make_async_copy(head, head, h_sem).wait()

    @pl.when(dp == 0)
    def _():
        tok[0:HALO, :] = jnp.zeros((HALO, D), jnp.bfloat16)

    def rows_of(chunk, start, size):
        return panel_dt.at[pl.ds(start, size)] if chunk == "dt" else panel.at[chunk, pl.ds(start, size)]

    def sem_of(chunk):
        return 5 if chunk == "dt" else chunk

    def block(chunk, zh_, x_, core_):
        return rows_of(chunk, dp_of(zh_, x_, core_) * KB, KB)

    def prepare(chunk):
        mine = dp * KB + ten * KR
        dst = rows_of(chunk, mine, KR)
        sem = a2a_sem.at[sem_of(chunk)]

        def source(slot):
            return stage_dt.at[slot] if chunk == "dt" else stage.at[chunk, slot]

        for step in range(1, 8):
            slot = (ten + step) % 8
            remote(source(slot), dst, send_sem.at[sem_of(chunk)], sem, (dp, slot)).start()
        pltpu.make_async_copy(source(ten), dst, sem).start()

    def send(chunk, ref, recv, peer):
        remote(ref, ref, send_sem.at[sem_of(chunk)], recv.at[sem_of(chunk)], peer).start()

    def wait(chunk, ref, sem):
        pltpu.make_async_copy(ref, ref, sem.at[sem_of(chunk)]).wait()

    def ring(kind):
        return ring_sem.at[kind]

    RL0, RR0, RL1, RR1, RO0, RO1 = range(6)

    def s_own(chunk):
        ref = block(chunk, zh, x, core)
        wait(chunk, ref, a2a_sem)
        send(chunk, ref, z_sem, at_zh)
        send(chunk, ref, ring(RL0), at_right)
        send(chunk, ref, ring(RR0), at_left)
        send(chunk, ref, sib_sem, at_sib)

    def s_pair(chunk):
        ref = block(chunk, 1 - zh, x, core)
        wait(chunk, ref, z_sem)
        send(chunk, ref, ring(RL1), at_right)
        send(chunk, ref, ring(RR1), at_left)
        send(chunk, ref, sib_sem, at_sib)

    def s_near(chunk):
        ref = block(chunk, zh, left, core)
        wait(chunk, ref, ring(RL0))
        send(chunk, ref, ring(RO0), at_right)
        send(chunk, ref, sib_sem, at_sib)
        ref = block(chunk, zh, right, core)
        wait(chunk, ref, ring(RR0))
        send(chunk, ref, sib_sem, at_sib)

    def s_next(chunk):
        ref = block(chunk, 1 - zh, right, core)
        wait(chunk, ref, ring(RR1))
        send(chunk, ref, ring(RO1), at_left)
        send(chunk, ref, sib_sem, at_sib)
        ref = block(chunk, 1 - zh, left, core)
        wait(chunk, ref, ring(RL1))
        send(chunk, ref, sib_sem, at_sib)

    def s_far(chunk):
        ref = block(chunk, zh, opposite, core)
        wait(chunk, ref, ring(RO0))
        send(chunk, ref, sib_sem, at_sib)
        ref = block(chunk, 1 - zh, opposite, core)
        wait(chunk, ref, ring(RO1))
        send(chunk, ref, sib_sem, at_sib)

    def s_sib(chunk):
        wait(chunk, rows_of(chunk, 0, 8 * KB), sib_sem)

    def silu(v):
        return 0.5 * v * (1.0 + jnp.tanh(0.5 * v))

    def rounded(v):
        return v.astype(jnp.bfloat16).astype(jnp.float32)

    def conv(taps, col):
        total = taps[0:1, :] * proj[pl.ds(HALO - 3, GRP), col : col + 256]
        for k in range(1, 4):
            total = total + taps[k : k + 1, :] * proj[pl.ds(HALO - 3 + k, GRP), col : col + 256]
        return total

    def multiply(group, chunk):
        start = pl.multiple_of(group * GRP, GRP)
        lhs = tok[pl.ds(start, HALO + GRP), :]
        for half in range(2):
            cols = slice(256 * half, 256 * half + 256)
            proj[:, cols] = rounded(jnp.dot(lhs, panel[chunk, :, cols], preferred_element_type=jnp.float32))

    def unit(group, chunk):
        multiply(group, chunk)
        start = pl.multiple_of(group * GRP, GRP)
        if chunk == 4:
            for half in range(2):
                cols = slice(256 * half, 256 * half + 256)
                states_v[pl.ds(start, GRP), cols] = silu(conv(conv_bc[:, cols], 256 * half)).astype(jnp.bfloat16)
            src = states_v.at[pl.ds(start, GRP)]
            dst = states.at[pl.ds(start, GRP)]
        else:
            cols = slice(256 * chunk, 256 * chunk + 256)
            value = silu(conv(conv_x[:, cols], 256)) * silu(proj[pl.ds(HALO, GRP), 0:256])
            gated_v[pl.ds(start, GRP), cols] = value.astype(jnp.bfloat16)
            src = gated_v.at[pl.ds(start, GRP), cols]
            dst = gated.at[pl.ds(start, GRP), cols]
        pltpu.make_async_copy(src, dst, out_sem).start()

    def unit_dt(group):
        start = pl.multiple_of(group * GRP, GRP)
        raw = rounded(jnp.dot(tok[pl.ds(start + HALO, GRP), :], panel_dt[...], preferred_element_type=jnp.float32))
        value = raw[:, :HPG] + dt_bias[...]
        steps[pl.ds(start, GRP), :] = jnp.maximum(value, 0.0) + jnp.log1p(jnp.exp(-jnp.abs(value)))

    def units(first, count, chunk):
        def body(step, carry):
            group = (y + first + step) % 4
            if chunk == "dt":
                unit_dt(group)
            else:
                unit(group, chunk)
            return carry

        lax.fori_loop(0, count, body, 0)

    pl.semaphore_wait(barrier, 13)
    own_t = tok_rows(y, zl)
    tok_send(tokens, own_t, ZL, at_zl)
    tok_send(tokens, own_t, L0, at_up)
    tok_send(tokens, own_t, R0, at_down)
    prepare("dt")
    prepare(0)
    s_own("dt")
    prepare(1)
    for k, chunk in enumerate(ORDER):
        s_pair(chunk)
        s_near(chunk)
        if k + 3 < 6:
            prepare(ORDER[k + 3])
        if k + 1 < 6:
            s_own(ORDER[k + 1])
        if k == 3:
            tok_next()
            halo_send(jnp.logical_or(y == 0, y == 2))
        s_next(chunk)
        if k >= 1:
            s_far(ORDER[k - 1])
            s_sib(ORDER[k - 1])
        if k == 1:
            tok_pair()
            tok_near()
            load_t.wait()
            halo_send(y == 3)
        if k == 3:
            halo_wait(jnp.logical_or(y == 0, y == 3))
            units(0, 2, 0)
            units(0, 2, 1)
        if k == 4:
            units(0, 2, 2)
        if k == 5:
            tok_far()
            halo_send(y == 1)
            units(0, 4, "dt")
            halo_wait(jnp.logical_or(y == 1, y == 2))
            for done in range(3):
                units(2, 2, done)
            units(0, 4, 3)
    s_far(4)
    s_sib(4)
    units(0, 4, 4)

    pltpu.make_async_copy(gated_v, gated, out_sem).wait()
    pltpu.make_async_copy(states_v, states, out_sem).wait()
    pltpu.make_async_copy(tok.at[pl.ds(0, 7 * TOK)], tok.at[pl.ds(0, 7 * TOK)], t_send).wait()

    @pl.when(dp < 15)
    def _():
        pltpu.make_async_copy(tail, tail, h_send).wait()

    for chunk in ORDER:
        ref = rows_of(chunk, 0, 15 * KB + 7 * KR)
        wait(chunk, ref, send_sem)


def on_device(tokens, in_weight, group_order, head_order, conv_x, conv_bc, dt_bias):
    vmem, smem, anywhere = (
        pl.BlockSpec(memory_space=pltpu.VMEM),
        pl.BlockSpec(memory_space=pltpu.SMEM),
        pl.BlockSpec(memory_space=pl.ANY),
    )
    dma = pltpu.SemaphoreType.DMA
    bf16, f32 = jnp.bfloat16, jnp.float32
    stage, stage_dt = pl.pallas_call(
        arrange,
        out_shape=(
            jax.ShapeDtypeStruct((5, 8, KR, CW), bf16),
            jax.ShapeDtypeStruct((8, KR, 128), bf16),
        ),
        in_specs=[smem, smem, vmem],
        out_specs=(vmem, vmem),
        scratch_shapes=[pltpu.VMEM((KR, 2688), f32)],
        compiler_params=pltpu.CompilerParams(vmem_limit_bytes=32 << 20),
        cost_estimate=pl.CostEstimate(flops=1 << 20, bytes_accessed=3 << 20, transcendentals=0),
    )(group_order, head_order, in_weight)
    return pl.pallas_call(
        kernel,
        out_shape=(
            jax.ShapeDtypeStruct((ROWS, HPG * HEAD), bf16),
            jax.ShapeDtypeStruct((ROWS, 2 * N), bf16),
            jax.ShapeDtypeStruct((ROWS, HPG), f32),
        ),
        in_specs=[anywhere, anywhere, anywhere, vmem, vmem, vmem],
        out_specs=(anywhere, anywhere, vmem),
        scratch_shapes=[
            pltpu.VMEM((5, D, CW), bf16),
            pltpu.VMEM((D, 128), bf16),
            pltpu.VMEM((HALO + ROWS, D), bf16),
            pltpu.VMEM((HALO + GRP, CW), f32),
            pltpu.VMEM((ROWS, HPG * HEAD), bf16),
            pltpu.VMEM((ROWS, 2 * N), bf16),
            dma((6,)), dma((6,)), dma((6, 6)), dma((6,)), dma((6,)), dma((7,)), dma, dma, dma, dma, dma,
        ],
        compiler_params=pltpu.CompilerParams(
            collective_id=0, has_side_effects=True, vmem_limit_bytes=56 << 20
        ),
        cost_estimate=pl.CostEstimate(
            flops=2 * ROWS * D * GW, bytes_accessed=6 << 20, transcendentals=ROWS * GW
        ),
    )(tokens, stage, stage_dt, conv_x, conv_bc, dt_bias.reshape(1, HPG))


def solution(mesh):
    return jax.shard_map(
        on_device,
        mesh=mesh,
        in_specs=(
            P(("dp", "tensor"), None),
            P(("dp", "tensor"), None),
            P(),
            P(),
            P(None, "tensor"),
            P(None, "tensor"),
            P("tensor"),
        ),
        out_specs=(P("dp", "tensor"), P("dp", "tensor"), P("dp", "tensor")),
        check_vma=False,
    )
```

time: 603 us -> 177 us (0.29)
  waiting for transfers between devices: 528 us -> 0 us
  Pallas kernels: 0 us -> 165 us
  matrix products: 27.7 us -> 0 us
  between operations: 14.6 us -> 0.67 us
  other arithmetic: 11.7 us -> 0 us
    all_gather x3 -> x0, waiting for transfers between devices: 527 us -> none  [the longest x1 209 us: on_device(): trainer_block = lax.all_gather(in_weight, 'tensor', axis=0, tiled=True)]
    pallas_call x0 -> x2, Pallas kernels: none -> 165 us  [the longest x1 162 us: on_device(): pl.pallas_call(kernel, out_shape=(jax.ShapeDtypeStruct((ROWS, HPG * HEAD)...]
    dot_general x1 -> x0, matrix products: 27.7 us -> none  [on_device(): jnp.dot(group_tokens, lax.all_gather(column_block, 'dp', axis=0, tiled=Tr...]
  transfers between devices with their start and end apart: 4 -> 0, of which waited for: 4 -> 0; matrix products, arithmetic and copies ran while one was open for 2% -> 0% of each run, Pallas kernels for 0% -> 0%
where the time goes in v1:
time: 177 us; the launch traced here: 176 us
  Pallas kernels  165 us (93%)
  local copies, waits for them, and re-layouts  10.3 us (6%)
    pallas_call x1, Pallas kernels, on_device(): pl.pallas_call(kernel, out_shape=(jax.ShapeDtypeStruct((ROWS, HPG * HEAD)...  162 us
    unnamed x14, local copies, waits for them, and re-layouts  8.47 us

profile of v1, /device:TPU:0, one launch (start us, length us, event | category | flops | bytes accessed | tf_op | source)
XLA Modules:
  0.0 175.7 jit_solution(6255743455850229494)
XLA Ops:
  0.6 0.0 copy-start
  0.6 1.3 copy-done
  2.0 0.0 copy-start.1
  2.0 0.7 copy-done.1
  2.6 0.0 copy-start.2
  2.6 0.7 copy-done.2
  3.3 3.0 %shard_map.94 = (bf16[5,8,32,512]{3,2,1,0:T(8,128)(2,1)S(1)}, bf16[8,32,128]{2,1,0:T(8,128)(2,1)S(1)}) custom-call(s32[8]{0:T(128)S(1)} %copy-done.2, s32[8,16]{1,0:T(8,128)S(1)} %copy-done.1, bf16[32,20608]{1,0:T(8,128)(2,1)S(1)} %copy-done), custom_call_target="tpu_custom_call" | custom-call | flops 1048576 | bytes 3145728 | tf_op jit(solution)/shard_map/pallas_call | solution.py:370
  6.3 0.0 copy-start.3
  6.3 1.0 copy-done.3
  7.4 0.0 copy-start.4
  7.4 0.6 copy-done.4
  8.0 161.7 %shard_map.95 = (bf16[1024,1024]{1,0:T(8,128)(2,1)}, bf16[1024,512]{1,0:T(8,128)(2,1)}, f32[1024,16]{1,0:T(8,128)}) custom-call(bf16[128,4096]{1,0:T(8,128)(2,1)} %tokens.1, bf16[5,8,32,512]{3,2,1,0:T(8,128)(2,1)} %copy-done.3, bf16[8,32,128]{2,1,0:T(8,128)(2,1)} %copy-done.4, f32[4,1024]{1,0:T(4,128)} %conv_x.1, f32[4,512]{1,0:T(4,128)} %conv_bc.1, ...), custom_call_target="tpu_custom_call" | custom-call | flops 21609054208 | bytes 6291456 | tf_op jit(solution)/shard_map/pallas_call | solution.py:382
  169.7 1.8 %copy.10 = f32[1024,16]{0,1:T(8,128)} copy(f32[1024,16]{1,0:T(8,128)} %get-tuple-element.9) | data formatting | bytes 131072 | tf_op jit(solution)/shard_map/pallas_call | solution.py:382
  171.6 0.0 copy-start.5
  171.6 3.2 %copy.13 = bf16[1024,1024]{1,0:T(8,128)(2,1)} copy(bf16[1024,1024]{1,0:T(8,128)(2,1)} %get-tuple-element.13) | data formatting | bytes 4194304
  174.7 0.0 copy-done.5
  174.8 1.0 copy.14
Async XLA Ops:
  0.6 1.3 copy-start
  2.0 0.7 copy-start.1
  2.6 0.7 copy-start.2
  6.3 1.1 copy-start.3
  7.4 0.6 copy-start.4
  171.6 3.2 %copy-start.5 = (bf16[1024,512]{1,0:T(8,128)(2,1)S(1)}, bf16[1024,512]{1,0:T(8,128)(2,1)}, u32[]{:S(2)}) copy-start(bf16[1024,512]{1,0:T(8,128)(2,1)} %get-tuple-element.14) | copy-start | bytes 3145732

commit v2 on v1

--- a/solution.py
+++ b/solution.py
@@ -15,25 +15,34 @@
 D = 4096
 ROWS = 1024
 TOK = 128
+PIECES = 4
+PIECE = TOK // PIECES
+HALF = {"b": slice(0, 256), "c": slice(256, 512)}
 KB = 256
 KR = 32
 GRP = 256
 HALO = 16
 CW = 512
-ORDER = ("dt", 0, 1, 2, 3, 4)
-
-
-def arrange(group_order, head_order, w_own, stage, stage_dt, lined):
+ORDER = ("dt", 0, 1, 2, 3, "b", "c")
+
+
+def arrange(group_order, head_order, weight, stage, stage_dt, held, lined, sems):
+    def fetch(slot):
+        start = pl.multiple_of(20 * 128 * group_order[slot], 128)
+        return pltpu.make_async_copy(weight.at[:, pl.ds(start, 2688)], held.at[slot], sems.at[slot])
+
+    for slot in range(8):
+        fetch(slot).start()
+
     lane = lax.broadcasted_iota(jnp.int32, (KR, 128), 1)
 
     def line_up(slot):
         group = group_order[slot]
+        fetch(slot).wait()
         for part in range(4):
-            start = pl.multiple_of((20 * group + 5 * part) * 128, 128)
-            wide = pltpu.roll(w_own[:, pl.ds(start, 768)].astype(jnp.float32), (768 - 16 * group) % 768, 1)
-            lined[:, 640 * part : 640 * part + 640] = wide[:, :640]
-        start = pl.multiple_of((20 * group + 20) * 128, 128)
-        tile = pltpu.roll(w_own[:, pl.ds(start, 128)].astype(jnp.float32), (128 - 16 * group) % 128, 1)
+            wide = held[slot, :, 640 * part : 640 * part + 768].astype(jnp.float32)
+            lined[:, 640 * part : 640 * part + 640] = pltpu.roll(wide, (768 - 16 * group) % 768, 1)[:, :640]
+        tile = pltpu.roll(held[slot, :, 2560:2688].astype(jnp.float32), (128 - 16 * group) % 128, 1)
         lined[:, 2560:2688] = jnp.where(lane < HPG, tile, 0.0)
 
     def head_tile(slot, base, first):
@@ -84,8 +93,8 @@
 def kernel(
     tokens, stage, stage_dt, conv_x, conv_bc, dt_bias,
     gated, states, steps,
-    panel, panel_dt, tok, proj, gated_v, states_v,
-    a2a_sem, z_sem, ring_sem, sib_sem, send_sem, t_sem, t_send, h_sem, h_send, own_sem, out_sem,
+    panel, panel_dt, tok, proj,
+    a2a_sem, z_sem, ring_sem, sib_sem, send_sem, t_sem, t_send, h_sem, h_send, own_sem,
 ):
     dp, ten = lax.axis_index("dp"), lax.axis_index("tensor")
     core, x, zh = dp % 2, (dp // 2) % 4, dp // 8
@@ -119,39 +128,54 @@
             src_ref=src, dst_ref=dst, send_sem=send, recv_sem=recv, device_id=peer, device_id_type=MESH
         )
 
-    def tok_rows(y_, zl_):
-        return tok.at[pl.ds(HALO + (y_ * 2 + zl_) * TOK, TOK)]
-
-    def tok_send(src, dst, sem, peer):
-        remote(src, dst, t_send, t_sem.at[sem], peer).start()
-
-    def tok_wait(sem, y_, zl_):
-        ref = tok_rows(y_, zl_)
-        pltpu.make_async_copy(ref, ref, t_sem.at[sem]).wait()
+    def tok_rows(y_, zl_, piece):
+        return tok.at[pl.ds(HALO + (y_ * 2 + zl_) * TOK + piece * PIECE, PIECE)]
 
     ZL, L0, R0, L1, R1, O0, O1 = range(7)
-
-    def tok_pair():
-        tok_wait(ZL, y, 1 - zl)
-        ref = tok_rows(y, 1 - zl)
-        tok_send(ref, ref, L1, at_up)
-        tok_send(ref, ref, R1, at_down)
+    arrives = {
+        ZL: (y, 1 - zl), L0: (down, zl), R0: (up, zl), L1: (down, 1 - zl),
+        R1: (up, 1 - zl), O0: (far, zl), O1: (far, 1 - zl),
+    }
+    waited = set()
+
+    def tok_wait(*kinds, pieces=range(PIECES)):
+        for kind in kinds:
+            for piece in pieces:
+                if (kind, piece) not in waited:
+                    waited.add((kind, piece))
+                    ref = tok_rows(*arrives[kind], piece)
+                    pltpu.make_async_copy(ref, ref, t_sem.at[kind, piece]).wait()
+
+    def tok_send(ref, dst, kind, piece, peer):
+        remote(ref, dst, t_send, t_sem.at[kind, piece], peer).start()
+
+    def slot(q):
+        piece = PIECES - 1 - q % PIECES
+        if q < PIECES:
+            src, dst = tokens.at[pl.ds(piece * PIECE, PIECE)], tok_rows(y, zl, piece)
+            tok_send(src, dst, L0, piece, at_up)
+            tok_send(src, dst, R0, piece, at_down)
+        elif q < 2 * PIECES:
+            tok_wait(ZL, pieces=(piece,))
+            ref = tok_rows(y, 1 - zl, piece)
+            tok_send(ref, ref, L1, piece, at_up)
+            tok_send(ref, ref, R1, piece, at_down)
+        else:
+            tok_wait(L0, R1, pieces=(piece,))
+            ref = tok_rows(down, zl, piece)
+            tok_send(ref, ref, O0, piece, at_up)
+            ref = tok_rows(up, 1 - zl, piece)
+            tok_send(ref, ref, O1, piece, at_down)
+
+    def across(piece):
+        src, dst = tokens.at[pl.ds(piece * PIECE, PIECE)], tok_rows(y, zl, piece)
+        tok_send(src, dst, ZL, piece, at_zl)
 
     def tok_near():
-        tok_wait(L0, down, zl)
-        ref = tok_rows(down, zl)
-        tok_send(ref, ref, O0, at_up)
-        tok_wait(R0, up, zl)
-
-    def tok_next():
-        tok_wait(R1, up, 1 - zl)
-        ref = tok_rows(up, 1 - zl)
-        tok_send(ref, ref, O1, at_down)
-        tok_wait(L1, down, 1 - zl)
+        tok_wait(ZL, L0, R0, L1, R1)
 
     def tok_far():
-        tok_wait(O0, far, zl)
-        tok_wait(O1, far, 1 - zl)
+        tok_wait(O0, O1)
 
     tail = tok.at[pl.ds(ROWS, HALO)]
     head = tok.at[pl.ds(0, HALO)]
@@ -171,10 +195,14 @@
         tok[0:HALO, :] = jnp.zeros((HALO, D), jnp.bfloat16)
 
     def rows_of(chunk, start, size):
-        return panel_dt.at[pl.ds(start, size)] if chunk == "dt" else panel.at[chunk, pl.ds(start, size)]
+        if chunk == "dt":
+            return panel_dt.at[pl.ds(start, size)]
+        if chunk in ("b", "c"):
+            return panel.at[4, pl.ds(start, size), HALF[chunk]]
+        return panel.at[chunk, pl.ds(start, size)]
 
     def sem_of(chunk):
-        return 5 if chunk == "dt" else chunk
+        return ORDER.index(chunk)
 
     def block(chunk, zh_, x_, core_):
         return rows_of(chunk, dp_of(zh_, x_, core_) * KB, KB)
@@ -185,7 +213,11 @@
         sem = a2a_sem.at[sem_of(chunk)]
 
         def source(slot):
-            return stage_dt.at[slot] if chunk == "dt" else stage.at[chunk, slot]
+            if chunk == "dt":
+                return stage_dt.at[slot]
+            if chunk in ("b", "c"):
+                return stage.at[4, slot, :, HALF[chunk]]
+            return stage.at[chunk, slot]
 
         for step in range(1, 8):
             slot = (ten + step) % 8
@@ -259,95 +291,138 @@
             total = total + taps[k : k + 1, :] * proj[pl.ds(HALO - 3 + k, GRP), col : col + 256]
         return total
 
-    def multiply(group, chunk):
+    def unit(group, chunk):
         start = pl.multiple_of(group * GRP, GRP)
         lhs = tok[pl.ds(start, HALO + GRP), :]
-        for half in range(2):
-            cols = slice(256 * half, 256 * half + 256)
-            proj[:, cols] = rounded(jnp.dot(lhs, panel[chunk, :, cols], preferred_element_type=jnp.float32))
-
-    def unit(group, chunk):
-        multiply(group, chunk)
-        start = pl.multiple_of(group * GRP, GRP)
-        if chunk == 4:
-            for half in range(2):
-                cols = slice(256 * half, 256 * half + 256)
-                states_v[pl.ds(start, GRP), cols] = silu(conv(conv_bc[:, cols], 256 * half)).astype(jnp.bfloat16)
-            src = states_v.at[pl.ds(start, GRP)]
-            dst = states.at[pl.ds(start, GRP)]
+        if chunk in ("b", "c"):
+            cols = HALF[chunk]
+            proj[:, 256:512] = rounded(jnp.dot(lhs, panel[4, :, cols], preferred_element_type=jnp.float32))
+            states[pl.ds(start, GRP), cols] = silu(conv(conv_bc[:, cols], 256)).astype(jnp.bfloat16)
         else:
+            for half in HALF.values():
+                proj[:, half] = rounded(jnp.dot(lhs, panel[chunk, :, half], preferred_element_type=jnp.float32))
             cols = slice(256 * chunk, 256 * chunk + 256)
             value = silu(conv(conv_x[:, cols], 256)) * silu(proj[pl.ds(HALO, GRP), 0:256])
-            gated_v[pl.ds(start, GRP), cols] = value.astype(jnp.bfloat16)
-            src = gated_v.at[pl.ds(start, GRP), cols]
-            dst = gated.at[pl.ds(start, GRP), cols]
-        pltpu.make_async_copy(src, dst, out_sem).start()
+            gated[pl.ds(start, GRP), cols] = value.astype(jnp.bfloat16)
 
     def unit_dt(group):
         start = pl.multiple_of(group * GRP, GRP)
         raw = rounded(jnp.dot(tok[pl.ds(start + HALO, GRP), :], panel_dt[...], preferred_element_type=jnp.float32))
-        value = raw[:, :HPG] + dt_bias[...]
-        steps[pl.ds(start, GRP), :] = jnp.maximum(value, 0.0) + jnp.log1p(jnp.exp(-jnp.abs(value)))
-
-    def units(first, count, chunk):
+        value = (raw[:, :HPG] + dt_bias[...]).T
+        steps[:, pl.ds(start, GRP)] = jnp.maximum(value, 0.0) + jnp.log1p(jnp.exp(-jnp.abs(value)))
+
+    def units(places, *chunks):
         def body(step, carry):
-            group = (y + first + step) % 4
-            if chunk == "dt":
-                unit_dt(group)
-            else:
-                unit(group, chunk)
+            group = groups[places[0]]
+            for index, place in enumerate(places[1:]):
+                group = jnp.where(step == index + 1, groups[place], group)
+            for chunk in chunks:
+                if chunk == "dt":
+                    unit_dt(group)
+                else:
+                    unit(group, chunk)
             return carry
 
-        lax.fori_loop(0, count, body, 0)
+        if len(places) == 1:
+            body(0, 0)
+        else:
+            lax.fori_loop(0, len(places), body, 0)
+
+    ends = jnp.logical_or(y == 0, y == 3)
+    groups = (
+        jnp.where(y == 3, 3, up),
+        jnp.where(ends, down, y),
+        jnp.where(ends, 0, down),
+        far,
+    )
 
     pl.semaphore_wait(barrier, 13)
-    own_t = tok_rows(y, zl)
-    tok_send(tokens, own_t, ZL, at_zl)
-    tok_send(tokens, own_t, L0, at_up)
-    tok_send(tokens, own_t, R0, at_down)
     prepare("dt")
     prepare(0)
+    slot(0)
     s_own("dt")
+    s_own(0)
     prepare(1)
-    for k, chunk in enumerate(ORDER):
-        s_pair(chunk)
-        s_near(chunk)
-        if k + 3 < 6:
-            prepare(ORDER[k + 3])
-        if k + 1 < 6:
-            s_own(ORDER[k + 1])
-        if k == 3:
-            tok_next()
-            halo_send(jnp.logical_or(y == 0, y == 2))
-        s_next(chunk)
-        if k >= 1:
-            s_far(ORDER[k - 1])
-            s_sib(ORDER[k - 1])
-        if k == 1:
-            tok_pair()
-            tok_near()
-            load_t.wait()
-            halo_send(y == 3)
-        if k == 3:
-            halo_wait(jnp.logical_or(y == 0, y == 3))
-            units(0, 2, 0)
-            units(0, 2, 1)
-        if k == 4:
-            units(0, 2, 2)
-        if k == 5:
-            tok_far()
-            halo_send(y == 1)
-            units(0, 4, "dt")
-            halo_wait(jnp.logical_or(y == 1, y == 2))
-            for done in range(3):
-                units(2, 2, done)
-            units(0, 4, 3)
-    s_far(4)
-    s_sib(4)
-    units(0, 4, 4)
-
-    pltpu.make_async_copy(gated_v, gated, out_sem).wait()
-    pltpu.make_async_copy(states_v, states, out_sem).wait()
+    across(3)
+    slot(1)
+    s_pair("dt")
+    s_near("dt")
+    across(2)
+    slot(2)
+    prepare(2)
+    s_next("dt")
+    s_pair(0)
+    s_own(1)
+    s_near(0)
+    across(1)
+    slot(3)
+    s_next(0)
+    s_far("dt")
+    across(0)
+    slot(4)
+    load_t.wait()
+    halo_send(y == 3)
+    s_pair(1)
+    s_own(2)
+    s_near(1)
+    slot(5)
+    prepare(3)
+    s_next(1)
+    slot(6)
+    s_far(0)
+    slot(7)
+    prepare("b")
+    prepare("c")
+    s_pair(2)
+    s_own(3)
+    s_near(2)
+    slot(8)
+    tok_wait(R0, L1, pieces=(3,))
+    halo_send(jnp.logical_or(y == 0, y == 2))
+    s_next(2)
+    slot(9)
+    s_far(1)
+    slot(10)
+    tok_wait(L0, R0, L1, R1)
+    s_sib("dt")
+    s_sib(0)
+    units((0,), "dt", 0)
+    s_pair(3)
+    s_own("b")
+    slot(11)
+    s_sib(1)
+    units((0,), 1)
+    s_near(3)
+    s_own("c")
+    tok_wait(O0, O1, pieces=(3,))
+    halo_send(y == 1)
+    units((1,), "dt", 0, 1)
+    s_next(3)
+    s_far(2)
+    halo_wait(y != 2)
+    units((2,), "dt", 0, 1)
+    s_pair("b")
+    s_near("b")
+    s_sib(2)
+    units((0, 1, 2), 2)
+    s_next("b")
+    s_far(3)
+    s_pair("c")
+    s_near("c")
+    tok_far()
+    halo_wait(y == 2)
+    units((3,), "dt", 0)
+    s_next("c")
+    units((3,), 1, 2)
+    s_far("b")
+    s_sib(3)
+    units((0, 1, 2, 3), 3)
+    s_far("c")
+    s_sib("b")
+    units((0, 1, 2, 3), "b")
+    s_sib("c")
+    units((0, 1, 2, 3), "c")
+
     pltpu.make_async_copy(tok.at[pl.ds(0, 7 * TOK)], tok.at[pl.ds(0, 7 * TOK)], t_send).wait()
 
     @pl.when(dp < 15)
@@ -357,6 +432,20 @@
     for chunk in ORDER:
         ref = rows_of(chunk, 0, 15 * KB + 7 * KR)
         wait(chunk, ref, send_sem)
+
+
+def finish(gated_v, states_v, steps_v, gated, states, steps, sems):
+    copies = [pltpu.make_async_copy(steps_v, steps, sems.at[6])]
+    for part in range(4):
+        rows = pl.ds(GRP * part, GRP)
+        copies.append(pltpu.make_async_copy(gated_v.at[rows], gated.at[rows], sems.at[part]))
+    for part in range(2):
+        rows = pl.ds(2 * GRP * part, 2 * GRP)
+        copies.append(pltpu.make_async_copy(states_v.at[rows], states.at[rows], sems.at[4 + part]))
+    for copy in copies:
+        copy.start()
+    for copy in copies:
+        copy.wait()
 
 
 def on_device(tokens, in_weight, group_order, head_order, conv_x, conv_bc, dt_bias):
@@ -367,35 +456,36 @@
     )
     dma = pltpu.SemaphoreType.DMA
     bf16, f32 = jnp.bfloat16, jnp.float32
+    def at_vmem(value):
+        return pltpu.with_memory_space_constraint(value, pltpu.VMEM)
+
+    def at_hbm(value):
+        return pltpu.with_memory_space_constraint(value, pltpu.HBM)
+
     stage, stage_dt = pl.pallas_call(
         arrange,
-        out_shape=(
-            jax.ShapeDtypeStruct((5, 8, KR, CW), bf16),
-            jax.ShapeDtypeStruct((8, KR, 128), bf16),
-        ),
-        in_specs=[smem, smem, vmem],
+        out_shape=(pltpu.VMEM((5, 8, KR, CW), bf16), pltpu.VMEM((8, KR, 128), bf16)),
+        in_specs=[smem, smem, anywhere],
         out_specs=(vmem, vmem),
-        scratch_shapes=[pltpu.VMEM((KR, 2688), f32)],
+        scratch_shapes=[pltpu.VMEM((8, KR, 2688), bf16), pltpu.VMEM((KR, 2688), f32), dma((8,))],
         compiler_params=pltpu.CompilerParams(vmem_limit_bytes=32 << 20),
         cost_estimate=pl.CostEstimate(flops=1 << 20, bytes_accessed=3 << 20, transcendentals=0),
-    )(group_order, head_order, in_weight)
-    return pl.pallas_call(
+    )(at_hbm(group_order), at_hbm(head_order), at_hbm(in_weight))
+    gated, states, steps = pl.pallas_call(
         kernel,
         out_shape=(
-            jax.ShapeDtypeStruct((ROWS, HPG * HEAD), bf16),
-            jax.ShapeDtypeStruct((ROWS, 2 * N), bf16),
-            jax.ShapeDtypeStruct((ROWS, HPG), f32),
+            pltpu.VMEM((ROWS, HPG * HEAD), bf16),
+            pltpu.VMEM((ROWS, 2 * N), bf16),
+            pltpu.VMEM((HPG, ROWS), f32),
         ),
-        in_specs=[anywhere, anywhere, anywhere, vmem, vmem, vmem],
-        out_specs=(anywhere, anywhere, vmem),
+        in_specs=[anywhere, vmem, vmem, vmem, vmem, vmem],
+        out_specs=(vmem, vmem, vmem),
         scratch_shapes=[
             pltpu.VMEM((5, D, CW), bf16),
             pltpu.VMEM((D, 128), bf16),
             pltpu.VMEM((HALO + ROWS, D), bf16),
             pltpu.VMEM((HALO + GRP, CW), f32),
-            pltpu.VMEM((ROWS, HPG * HEAD), bf16),
-            pltpu.VMEM((ROWS, 2 * N), bf16),
-            dma((6,)), dma((6,)), dma((6, 6)), dma((6,)), dma((6,)), dma((7,)), dma, dma, dma, dma, dma,
+            dma((7,)), dma((7,)), dma((6, 7)), dma((7,)), dma((7,)), dma((7, PIECES)), dma, dma, dma, dma,
         ],
         compiler_params=pltpu.CompilerParams(
             collective_id=0, has_side_effects=True, vmem_limit_bytes=56 << 20
@@ -403,7 +493,20 @@
         cost_estimate=pl.CostEstimate(
             flops=2 * ROWS * D * GW, bytes_accessed=6 << 20, transcendentals=ROWS * GW
         ),
-    )(tokens, stage, stage_dt, conv_x, conv_bc, dt_bias.reshape(1, HPG))
+    )(at_hbm(tokens), at_vmem(stage), at_vmem(stage_dt), conv_x, conv_bc, dt_bias.reshape(1, HPG))
+    gated, states, steps = pl.pallas_call(
+        finish,
+        out_shape=(
+            pltpu.HBM((ROWS, HPG * HEAD), bf16),
+            pltpu.HBM((ROWS, 2 * N), bf16),
+            pltpu.HBM((HPG, ROWS), f32),
+        ),
+        in_specs=[vmem, vmem, vmem],
+        out_specs=(anywhere, anywhere, anywhere),
+        scratch_shapes=[dma((7,))],
+        cost_estimate=pl.CostEstimate(flops=0, bytes_accessed=3 << 20, transcendentals=0),
+    )(at_vmem(gated), at_vmem(states), at_vmem(steps))
+    return gated, states, steps.T
 
 
 def solution(mesh):

time: 177 us -> 135 us (0.76)
  Pallas kernels: 165 us -> 132 us
  local copies, waits for them, and re-layouts: 10.3 us -> 0 us
    pallas_call x2 -> x3, Pallas kernels: 165 us -> 132 us  [the longest x1 126 us: on_device(): pl.pallas_call(kernel, out_shape=(pltpu.VMEM((ROWS, HPG * HEAD), bf16), p...]
    unnamed x14 -> x0, local copies, waits for them, and re-layouts: 8.47 us -> none
    pallas_call x1 -> x0, local copies, waits for them, and re-layouts: 1.84 us -> none  [on_device(): pl.pallas_call(kernel, out_shape=(jax.ShapeDtypeStruct((ROWS, HPG * HEAD)...]
where the time goes in v2:
time: 135 us; the launch traced here: 133 us
  Pallas kernels  132 us (98%)
    pallas_call x1, Pallas kernels, on_device(): pl.pallas_call(kernel, out_shape=(pltpu.VMEM((ROWS, HPG * HEAD), bf16), p...  126 us
    pallas_call x1, Pallas kernels, on_device(): pl.pallas_call(arrange, out_shape=(pltpu.VMEM((5, 8, KR, CW), bf16), pltp...  4.1 us

profile of v2, /device:TPU:0, one launch (start us, length us, event | category | flops | bytes accessed | tf_op | source)
XLA Modules:
  0.0 133.1 jit_solution(10689002065665348590)
XLA Ops:
  0.6 4.1 %shard_map.94 = (bf16[5,8,32,512]{3,2,1,0:T(8,128)(2,1)S(1)}, bf16[8,32,128]{2,1,0:T(8,128)(2,1)S(1)}) custom-call(s32[8]{0:T(128)} %group_order.1, s32[8,16]{1,0:T(8,128)} %head_order.1, bf16[32,20608]{1,0:T(8,128)(2,1)} %weight.1), custom_call_target="tpu_custom_call" | custom-call | flops 1048576 | bytes 3145728 | tf_op jit(solution)/shard_map/pallas_call | solution.py:465
  4.7 126.5 %shard_map.95 = (bf16[1024,1024]{1,0:T(8,128)(2,1)S(1)}, bf16[1024,512]{1,0:T(8,128)(2,1)S(1)}, f32[16,1024]{1,0:T(8,128)S(1)}) custom-call(bf16[128,4096]{1,0:T(8,128)(2,1)} %tokens.1, bf16[5,8,32,512]{3,2,1,0:T(8,128)(2,1)S(1)} %get-tuple-element.11.stage, bf16[8,32,128]{2,1,0:T(8,128)(2,1)S(1)} %get-tuple-element.12.stage_dt, f32[4,1024]{1,0:T(4,128)} %conv_x.1, ...), custom_call_target="tpu_custom_call" | custom-call | flops 21609054208 | bytes 6291456 | tf_op jit(solution)/shard_map/pallas_call | solution.py:474
  131.2 1.7 %shard_map.96 = (bf16[1024,1024]{1,0:T(8,128)(2,1)}, bf16[1024,512]{1,0:T(8,128)(2,1)}, f32[16,1024]{1,0:T(8,128)}) custom-call(bf16[1024,1024]{1,0:T(8,128)(2,1)S(1)} %get-tuple-element.13.gated_v, bf16[1024,512]{1,0:T(8,128)(2,1)S(1)} %get-tuple-element.14.states_v, f32[16,1024]{1,0:T(8,128)S(1)} %get-tuple-element.15.steps_v), custom_call_target="tpu_custom_call" | custom-call | bytes 3145728 | tf_op jit(solution)/shard_map/pallas_call | solution.py:497

commit v3 on v2

--- a/solution.py
+++ b/solution.py
@@ -24,6 +24,7 @@
 HALO = 16
 CW = 512
 ORDER = ("dt", 0, 1, 2, 3, "b", "c")
+BY_Z = ("b", "c")
 
 
 def arrange(group_order, head_order, weight, stage, stage_dt, held, lined, sems):
@@ -35,6 +36,7 @@
         fetch(slot).start()
 
     lane = lax.broadcasted_iota(jnp.int32, (KR, 128), 1)
+    ten = lax.axis_index("tensor")
 
     def line_up(slot):
         group = group_order[slot]
@@ -59,7 +61,7 @@
             source = jnp.full((128, 128), 128, jnp.int32)
             across = lax.broadcasted_iota(jnp.int32, (128, 128), 1)
             for j in range(HPG):
-                source = jnp.where(across == j, head_order[slot, j], source)
+                source = jnp.where(across == j + HPG * ten, head_order[slot, j], source)
             down = lax.broadcasted_iota(jnp.int32, (128, 128), 0)
             pick = (down == source).astype(jnp.float32).astype(jnp.bfloat16)
             tile = lined[:, 2560:2688].astype(jnp.bfloat16)
@@ -93,7 +95,7 @@
 def kernel(
     tokens, stage, stage_dt, conv_x, conv_bc, dt_bias,
     gated, states, steps,
-    panel, panel_dt, tok, proj,
+    panel, panel_dt, dt_in, dt_all, tok, proj,
     a2a_sem, z_sem, ring_sem, sib_sem, send_sem, t_sem, t_send, h_sem, h_send, own_sem,
 ):
     dp, ten = lax.axis_index("dp"), lax.axis_index("tensor")
@@ -177,26 +179,40 @@
     def tok_far():
         tok_wait(O0, O1)
 
-    tail = tok.at[pl.ds(ROWS, HALO)]
     head = tok.at[pl.ds(0, HALO)]
 
-    def halo_send(where):
-        @pl.when(jnp.logical_and(where, dp < 15))
+    def halo_send(where, src, *peers):
+        @pl.when(where)
         def _():
-            remote(tail, head, h_send, h_sem, after).start()
+            for peer in peers:
+                remote(src, head, h_send, h_sem, peer).start()
 
     def halo_wait(where):
         @pl.when(jnp.logical_and(where, dp > 0))
         def _():
             pltpu.make_async_copy(head, head, h_sem).wait()
 
+    def halo_sent(where, count):
+        @pl.when(where)
+        def _():
+            for _ in range(count):
+                pltpu.make_async_copy(head, head, h_send).wait()
+
+    halo_first = jnp.logical_and(ten == 7, dp < 15)
+    halo_a = ten == 7
+    halo_b = ten == 6
+    halo_c = ten == 1
+    halo_d = ten == 4
+    halo_rest = jnp.logical_or(jnp.logical_or(ten == 0, ten == 5), y == 1)
+    inner = dp > 0
+
     @pl.when(dp == 0)
     def _():
         tok[0:HALO, :] = jnp.zeros((HALO, D), jnp.bfloat16)
 
     def rows_of(chunk, start, size):
         if chunk == "dt":
-            return panel_dt.at[pl.ds(start, size)]
+            return dt_all.at[pl.ds(start, size)]
         if chunk in ("b", "c"):
             return panel.at[4, pl.ds(start, size), HALF[chunk]]
         return panel.at[chunk, pl.ds(start, size)]
@@ -204,12 +220,17 @@
     def sem_of(chunk):
         return ORDER.index(chunk)
 
+    def height(chunk):
+        return KR if chunk == "dt" else KB
+
     def block(chunk, zh_, x_, core_):
-        return rows_of(chunk, dp_of(zh_, x_, core_) * KB, KB)
+        return rows_of(chunk, dp_of(zh_, x_, core_) * height(chunk), height(chunk))
 
     def prepare(chunk):
-        mine = dp * KB + ten * KR
-        dst = rows_of(chunk, mine, KR)
+        if chunk == "dt":
+            dst, sent = dt_in.at[pl.ds(ten * KR, KR)], send_sem.at[len(ORDER)]
+        else:
+            dst, sent = rows_of(chunk, dp * KB + ten * KR, KR), send_sem.at[sem_of(chunk)]
         sem = a2a_sem.at[sem_of(chunk)]
 
         def source(slot):
@@ -221,7 +242,7 @@
 
         for step in range(1, 8):
             slot = (ten + step) % 8
-            remote(source(slot), dst, send_sem.at[sem_of(chunk)], sem, (dp, slot)).start()
+            remote(source(slot), dst, sent, sem, (dp, slot)).start()
         pltpu.make_async_copy(source(ten), dst, sem).start()
 
     def send(chunk, ref, recv, peer):
@@ -235,10 +256,21 @@
 
     RL0, RR0, RL1, RR1, RO0, RO1 = range(6)
 
+    def s_z(chunk):
+        send(chunk, block(chunk, zh, x, core), z_sem, at_zh)
+
+    def s_ready(chunk):
+        if chunk == "dt":
+            pltpu.make_async_copy(dt_in, dt_in, a2a_sem.at[sem_of(chunk)]).wait()
+            total = dt_in[0:KR, :].astype(jnp.float32)
+            for sender in range(1, 8):
+                total = total + dt_in[KR * sender : KR * sender + KR, :].astype(jnp.float32)
+            dt_all[pl.ds(dp * KR, KR), :] = total.astype(jnp.bfloat16)
+        else:
+            wait(chunk, block(chunk, zh, x, core), a2a_sem)
+
     def s_own(chunk):
         ref = block(chunk, zh, x, core)
-        wait(chunk, ref, a2a_sem)
-        send(chunk, ref, z_sem, at_zh)
         send(chunk, ref, ring(RL0), at_right)
         send(chunk, ref, ring(RR0), at_left)
         send(chunk, ref, sib_sem, at_sib)
@@ -246,17 +278,22 @@
     def s_pair(chunk):
         ref = block(chunk, 1 - zh, x, core)
         wait(chunk, ref, z_sem)
-        send(chunk, ref, ring(RL1), at_right)
-        send(chunk, ref, ring(RR1), at_left)
+        if chunk not in BY_Z:
+            send(chunk, ref, ring(RL1), at_right)
+            send(chunk, ref, ring(RR1), at_left)
         send(chunk, ref, sib_sem, at_sib)
 
     def s_near(chunk):
         ref = block(chunk, zh, left, core)
         wait(chunk, ref, ring(RL0))
         send(chunk, ref, ring(RO0), at_right)
+        if chunk in BY_Z:
+            send(chunk, ref, ring(RL1), at_zh)
         send(chunk, ref, sib_sem, at_sib)
         ref = block(chunk, zh, right, core)
         wait(chunk, ref, ring(RR0))
+        if chunk in BY_Z:
+            send(chunk, ref, ring(RR1), at_zh)
         send(chunk, ref, sib_sem, at_sib)
 
     def s_next(chunk):
@@ -277,7 +314,13 @@
         send(chunk, ref, sib_sem, at_sib)
 
     def s_sib(chunk):
-        wait(chunk, rows_of(chunk, 0, 8 * KB), sib_sem)
+        wait(chunk, rows_of(chunk, 0, 8 * height(chunk)), sib_sem)
+
+    def unpack():
+        packed = dt_all[...].astype(jnp.float32)
+        for sender in range(8):
+            turned = pltpu.roll(packed, (128 - HPG * sender) % 128, 1)
+            panel_dt[:, sender] = turned.reshape(16, KR, 128).astype(jnp.bfloat16)
 
     def silu(v):
         return 0.5 * v * (1.0 + jnp.tanh(0.5 * v))
@@ -285,29 +328,36 @@
     def rounded(v):
         return v.astype(jnp.bfloat16).astype(jnp.float32)
 
-    def conv(taps, col):
-        total = taps[0:1, :] * proj[pl.ds(HALO - 3, GRP), col : col + 256]
+    def conv(taps, size, col):
+        total = taps[0:1, :] * proj[pl.ds(HALO - 3, size), col : col + 256]
         for k in range(1, 4):
-            total = total + taps[k : k + 1, :] * proj[pl.ds(HALO - 3 + k, GRP), col : col + 256]
+            total = total + taps[k : k + 1, :] * proj[pl.ds(HALO - 3 + k, size), col : col + 256]
         return total
 
-    def unit(group, chunk):
-        start = pl.multiple_of(group * GRP, GRP)
-        lhs = tok[pl.ds(start, HALO + GRP), :]
+    def unit(start, size, chunk):
+        lhs = tok[pl.ds(start, HALO + size), :]
+        into = pl.ds(0, HALO + size)
         if chunk in ("b", "c"):
             cols = HALF[chunk]
-            proj[:, 256:512] = rounded(jnp.dot(lhs, panel[4, :, cols], preferred_element_type=jnp.float32))
-            states[pl.ds(start, GRP), cols] = silu(conv(conv_bc[:, cols], 256)).astype(jnp.bfloat16)
+            proj[into, 256:512] = rounded(jnp.dot(lhs, panel[4, :, cols], preferred_element_type=jnp.float32))
+            states[pl.ds(start, size), cols] = silu(conv(conv_bc[:, cols], size, 256)).astype(jnp.bfloat16)
         else:
             for half in HALF.values():
-                proj[:, half] = rounded(jnp.dot(lhs, panel[chunk, :, half], preferred_element_type=jnp.float32))
+                proj[into, half] = rounded(jnp.dot(lhs, panel[chunk, :, half], preferred_element_type=jnp.float32))
             cols = slice(256 * chunk, 256 * chunk + 256)
-            value = silu(conv(conv_x[:, cols], 256)) * silu(proj[pl.ds(HALO, GRP), 0:256])
-            gated[pl.ds(start, GRP), cols] = value.astype(jnp.bfloat16)
+            value = silu(conv(conv_x[:, cols], size, 256)) * silu(proj[pl.ds(HALO, size), 0:256])
+            gated[pl.ds(start, size), cols] = value.astype(jnp.bfloat16)
+
+    def whole(chunk):
+        def body(step, carry):
+            unit(pl.multiple_of(step * 2 * GRP, 2 * GRP), 2 * GRP, chunk)
+            return carry
+
+        lax.fori_loop(0, 2, body, 0)
 
     def unit_dt(group):
         start = pl.multiple_of(group * GRP, GRP)
-        raw = rounded(jnp.dot(tok[pl.ds(start + HALO, GRP), :], panel_dt[...], preferred_element_type=jnp.float32))
+        raw = rounded(jnp.dot(tok[pl.ds(start + HALO, GRP), :], panel_dt[...].reshape(D, 128), preferred_element_type=jnp.float32))
         value = (raw[:, :HPG] + dt_bias[...]).T
         steps[:, pl.ds(start, GRP)] = jnp.maximum(value, 0.0) + jnp.log1p(jnp.exp(-jnp.abs(value)))
 
@@ -320,7 +370,7 @@
                 if chunk == "dt":
                     unit_dt(group)
                 else:
-                    unit(group, chunk)
+                    unit(pl.multiple_of(group * GRP, GRP), GRP, chunk)
             return carry
 
         if len(places) == 1:
@@ -328,110 +378,130 @@
         else:
             lax.fori_loop(0, len(places), body, 0)
 
-    ends = jnp.logical_or(y == 0, y == 3)
-    groups = (
-        jnp.where(y == 3, 3, up),
-        jnp.where(ends, down, y),
-        jnp.where(ends, 0, down),
-        far,
-    )
+    groups = (y, up, down, far)
 
     pl.semaphore_wait(barrier, 13)
+    prepare(0)
+    halo_send(halo_first, tokens.at[pl.ds(TOK - HALO, HALO)], after)
+    prepare(1)
     prepare("dt")
-    prepare(0)
+    s_ready(0)
+    s_z(0)
+    s_own(0)
+    prepare(2)
     slot(0)
-    s_own("dt")
-    s_own(0)
-    prepare(1)
+    s_ready(1)
+    s_own(1)
+    s_near(0)
     across(3)
     slot(1)
-    s_pair("dt")
-    s_near("dt")
+    halo_wait(halo_a)
+    halo_send(jnp.logical_and(halo_a, inner), head, at_zl, at_up, at_down)
+    s_pair(0)
+    s_z(1)
+    s_ready("dt")
+    s_z("dt")
+    s_own("dt")
+    s_ready(2)
+    s_own(2)
+    prepare(3)
+    slot(2)
     across(2)
-    slot(2)
-    prepare(2)
-    s_next("dt")
-    s_pair(0)
-    s_own(1)
-    s_near(0)
+    s_next(0)
+    s_near(1)
     across(1)
     slot(3)
-    s_next(0)
-    s_far("dt")
+    halo_wait(halo_b)
+    halo_send(jnp.logical_and(halo_b, inner), head, at_up, at_down)
+    s_pair(1)
+    s_z(2)
+    slot(4)
+    prepare("b")
+    s_near("dt")
+    s_pair("dt")
+    s_ready(3)
+    s_own(3)
+    slot(5)
     across(0)
-    slot(4)
-    load_t.wait()
-    halo_send(y == 3)
-    s_pair(1)
-    s_own(2)
-    s_near(1)
-    slot(5)
-    prepare(3)
     s_next(1)
+    s_near(2)
+    s_far(0)
     slot(6)
-    s_far(0)
-    slot(7)
-    prepare("b")
     prepare("c")
     s_pair(2)
-    s_own(3)
-    s_near(2)
+    s_z(3)
+    halo_wait(jnp.logical_or(halo_c, halo_d))
+    halo_send(jnp.logical_and(halo_c, inner), head, at_up)
+    halo_send(jnp.logical_and(halo_d, inner), head, at_down)
+    s_ready("b")
+    s_own("b")
+    slot(7)
+    s_next("dt")
+    load_t.wait()
+    halo_wait(halo_rest)
+    tok_wait(ZL)
+    tok_wait(L0, L1, pieces=(3,))
+    s_sib(0)
+    units((0,), 0)
     slot(8)
-    tok_wait(R0, L1, pieces=(3,))
-    halo_send(jnp.logical_or(y == 0, y == 2))
     s_next(2)
+    s_near(3)
+    s_pair(3)
+    s_z("b")
+    s_far(1)
+    s_ready("c")
+    s_own("c")
     slot(9)
-    s_far(1)
+    s_sib(1)
+    units((0,), 1)
+    s_far("dt")
+    s_sib("dt")
+    unpack()
+    units((0,), "dt")
     slot(10)
     tok_wait(L0, R0, L1, R1)
-    s_sib("dt")
-    s_sib(0)
-    units((0,), "dt", 0)
-    s_pair(3)
-    s_own("b")
+    units((1,), "dt", 0, 1)
     slot(11)
-    s_sib(1)
-    units((0,), 1)
-    s_near(3)
-    s_own("c")
     tok_wait(O0, O1, pieces=(3,))
-    halo_send(y == 1)
-    units((1,), "dt", 0, 1)
+    units((2,), 0)
     s_next(3)
+    s_near("b")
+    s_pair("b")
+    s_z("c")
     s_far(2)
-    halo_wait(y != 2)
-    units((2,), "dt", 0, 1)
-    s_pair("b")
-    s_near("b")
     s_sib(2)
-    units((0, 1, 2), 2)
+    units((0, 1), 2)
     s_next("b")
+    s_near("c")
+    s_pair("c")
+    units((2,), "dt", 1, 2)
     s_far(3)
-    s_pair("c")
-    s_near("c")
-    tok_far()
-    halo_wait(y == 2)
-    units((3,), "dt", 0)
     s_next("c")
-    units((3,), 1, 2)
     s_far("b")
     s_sib(3)
-    units((0, 1, 2, 3), 3)
+    units((0, 1), 3)
     s_far("c")
+    units((2,), 3)
+    tok_far()
+    units((3,), "dt", 0, 1)
+    units((3,), 2, 3)
     s_sib("b")
-    units((0, 1, 2, 3), "b")
+    whole("b")
     s_sib("c")
-    units((0, 1, 2, 3), "c")
+    whole("c")
 
     pltpu.make_async_copy(tok.at[pl.ds(0, 7 * TOK)], tok.at[pl.ds(0, 7 * TOK)], t_send).wait()
 
-    @pl.when(dp < 15)
-    def _():
-        pltpu.make_async_copy(tail, tail, h_send).wait()
-
-    for chunk in ORDER:
-        ref = rows_of(chunk, 0, 15 * KB + 7 * KR)
-        wait(chunk, ref, send_sem)
+    halo_sent(halo_first, 1)
+    halo_sent(jnp.logical_and(halo_a, inner), 3)
+    halo_sent(jnp.logical_and(halo_b, inner), 2)
+    halo_sent(jnp.logical_and(jnp.logical_or(halo_c, halo_d), inner), 1)
+
+    for chunk in ORDER[1:]:
+        wait(chunk, rows_of(chunk, 0, 15 * KB + 7 * KR), send_sem)
+    wait("dt", rows_of("dt", 0, 15 * KR), send_sem)
+    ref = dt_in.at[pl.ds(0, 7 * KR)]
+    pltpu.make_async_copy(ref, ref, send_sem.at[len(ORDER)]).wait()
 
 
 def finish(gated_v, states_v, steps_v, gated, states, steps, sems):
@@ -482,10 +552,12 @@
         out_specs=(vmem, vmem, vmem),
         scratch_shapes=[
             pltpu.VMEM((5, D, CW), bf16),
-            pltpu.VMEM((D, 128), bf16),
+            pltpu.VMEM((16, 8, KR, 128), bf16),
+            pltpu.VMEM((8 * KR, 128), bf16),
+            pltpu.VMEM((16 * KR, 128), bf16),
             pltpu.VMEM((HALO + ROWS, D), bf16),
-            pltpu.VMEM((HALO + GRP, CW), f32),
-            dma((7,)), dma((7,)), dma((6, 7)), dma((7,)), dma((7,)), dma((7, PIECES)), dma, dma, dma, dma,
+            pltpu.VMEM((HALO + 2 * GRP, CW), f32),
+            dma((7,)), dma((7,)), dma((6, 7)), dma((7,)), dma((8,)), dma((7, PIECES)), dma, dma, dma, dma,
         ],
         compiler_params=pltpu.CompilerParams(
             collective_id=0, has_side_effects=True, vmem_limit_bytes=56 << 20

time: 135 us -> 126 us (0.933); the launches traced: 133 us -> 126 us
  Pallas kernels: 132 us -> 125 us
    pallas_call x1, Pallas kernels: 126 us -> 119 us  [on_device(): pl.pallas_call(kernel, out_shape=(pltpu.VMEM((ROWS, HPG * HEAD), bf16), p...]
where the time goes in v3:
time: 126 us
  Pallas kernels  125 us (99%)
    pallas_call x1, Pallas kernels, on_device(): pl.pallas_call(kernel, out_shape=(pltpu.VMEM((ROWS, HPG * HEAD), bf16), p...  119 us
    pallas_call x1, Pallas kernels, on_device(): pl.pallas_call(arrange, out_shape=(pltpu.VMEM((5, 8, KR, CW), bf16), pltp...  4.09 us

profile of v3, /device:TPU:0, one launch (start us, length us, event | category | flops | bytes accessed | tf_op | source)
XLA Modules:
  0.0 126.0 jit_solution(7158808174935468511)
XLA Ops:
  0.6 4.1 %shard_map.94 = (bf16[5,8,32,512]{3,2,1,0:T(8,128)(2,1)S(1)}, bf16[8,32,128]{2,1,0:T(8,128)(2,1)S(1)}) custom-call(s32[8]{0:T(128)} %group_order.1, s32[8,16]{1,0:T(8,128)} %head_order.1, bf16[32,20608]{1,0:T(8,128)(2,1)} %weight.1), custom_call_target="tpu_custom_call" | custom-call | flops 1048576 | bytes 3145728 | tf_op jit(solution)/shard_map/pallas_call | solution.py:535
  4.7 119.4 %shard_map.95 = (bf16[1024,1024]{1,0:T(8,128)(2,1)S(1)}, bf16[1024,512]{1,0:T(8,128)(2,1)S(1)}, f32[16,1024]{1,0:T(8,128)S(1)}) custom-call(bf16[128,4096]{1,0:T(8,128)(2,1)} %tokens.1, bf16[5,8,32,512]{3,2,1,0:T(8,128)(2,1)S(1)} %get-tuple-element.11.stage, bf16[8,32,128]{2,1,0:T(8,128)(2,1)S(1)} %get-tuple-element.12.stage_dt, f32[4,1024]{1,0:T(4,128)} %conv_x.1, ...), custom_call_target="tpu_custom_call" | custom-call | flops 21609054208 | bytes 6291456 | tf_op jit(solution)/shard_map/pallas_call | solution.py:544
  124.1 1.7 %shard_map.96 = (bf16[1024,1024]{1,0:T(8,128)(2,1)}, bf16[1024,512]{1,0:T(8,128)(2,1)}, f32[16,1024]{1,0:T(8,128)}) custom-call(bf16[1024,1024]{1,0:T(8,128)(2,1)S(1)} %get-tuple-element.13.gated_v, bf16[1024,512]{1,0:T(8,128)(2,1)S(1)} %get-tuple-element.14.states_v, f32[16,1024]{1,0:T(8,128)S(1)} %get-tuple-element.15.steps_v), custom_call_target="tpu_custom_call" | custom-call | bytes 3145728 | tf_op jit(solution)/shard_map/pallas_call | solution.py:569

commit v4 on v3

--- a/solution.py
+++ b/solution.py
@@ -24,7 +24,7 @@
 HALO = 16
 CW = 512
 ORDER = ("dt", 0, 1, 2, 3, "b", "c")
-BY_Z = ("b", "c")
+BY_Z = (3, "b")
 
 
 def arrange(group_order, head_order, weight, stage, stage_dt, held, lined, sems):
@@ -203,7 +203,8 @@
     halo_b = ten == 6
     halo_c = ten == 1
     halo_d = ten == 4
-    halo_rest = jnp.logical_or(jnp.logical_or(ten == 0, ten == 5), y == 1)
+    halo_e = ten == 0
+    halo_rest = jnp.logical_or(ten == 5, y == 1)
     inner = dp > 0
 
     @pl.when(dp == 0)
@@ -283,6 +284,13 @@
             send(chunk, ref, ring(RR1), at_left)
         send(chunk, ref, sib_sem, at_sib)
 
+    def s_right(chunk):
+        ref = block(chunk, zh, right, core)
+        wait(chunk, ref, ring(RR0))
+        if chunk in BY_Z:
+            send(chunk, ref, ring(RR1), at_zh)
+        send(chunk, ref, sib_sem, at_sib)
+
     def s_near(chunk):
         ref = block(chunk, zh, left, core)
         wait(chunk, ref, ring(RL0))
@@ -290,22 +298,21 @@
         if chunk in BY_Z:
             send(chunk, ref, ring(RL1), at_zh)
         send(chunk, ref, sib_sem, at_sib)
-        ref = block(chunk, zh, right, core)
-        wait(chunk, ref, ring(RR0))
         if chunk in BY_Z:
-            send(chunk, ref, ring(RR1), at_zh)
-        send(chunk, ref, sib_sem, at_sib)
+            s_right(chunk)
 
     def s_next(chunk):
         ref = block(chunk, 1 - zh, right, core)
         wait(chunk, ref, ring(RR1))
         send(chunk, ref, ring(RO1), at_left)
         send(chunk, ref, sib_sem, at_sib)
+
+    def s_far(chunk):
+        if chunk not in BY_Z:
+            s_right(chunk)
         ref = block(chunk, 1 - zh, left, core)
         wait(chunk, ref, ring(RL1))
         send(chunk, ref, sib_sem, at_sib)
-
-    def s_far(chunk):
         ref = block(chunk, zh, opposite, core)
         wait(chunk, ref, ring(RO0))
         send(chunk, ref, sib_sem, at_sib)
@@ -339,8 +346,9 @@
         into = pl.ds(0, HALO + size)
         if chunk in ("b", "c"):
             cols = HALF[chunk]
-            proj[into, 256:512] = rounded(jnp.dot(lhs, panel[4, :, cols], preferred_element_type=jnp.float32))
-            states[pl.ds(start, size), cols] = silu(conv(conv_bc[:, cols], size, 256)).astype(jnp.bfloat16)
+            spot = HALF["b" if (start // size) % 2 else "c"]
+            proj[into, spot] = rounded(jnp.dot(lhs, panel[4, :, cols], preferred_element_type=jnp.float32))
+            states[pl.ds(start, size), cols] = silu(conv(conv_bc[:, cols], size, spot.start)).astype(jnp.bfloat16)
         else:
             for half in HALF.values():
                 proj[into, half] = rounded(jnp.dot(lhs, panel[chunk, :, half], preferred_element_type=jnp.float32))
@@ -349,11 +357,8 @@
             gated[pl.ds(start, size), cols] = value.astype(jnp.bfloat16)
 
     def whole(chunk):
-        def body(step, carry):
-            unit(pl.multiple_of(step * 2 * GRP, 2 * GRP), 2 * GRP, chunk)
-            return carry
-
-        lax.fori_loop(0, 2, body, 0)
+        for step in range(2):
+            unit(step * 2 * GRP, 2 * GRP, chunk)
 
     def unit_dt(group):
         start = pl.multiple_of(group * GRP, GRP)
@@ -362,21 +367,12 @@
         steps[:, pl.ds(start, GRP)] = jnp.maximum(value, 0.0) + jnp.log1p(jnp.exp(-jnp.abs(value)))
 
     def units(places, *chunks):
-        def body(step, carry):
-            group = groups[places[0]]
-            for index, place in enumerate(places[1:]):
-                group = jnp.where(step == index + 1, groups[place], group)
+        for place in places:
             for chunk in chunks:
                 if chunk == "dt":
-                    unit_dt(group)
+                    unit_dt(groups[place])
                 else:
-                    unit(pl.multiple_of(group * GRP, GRP), GRP, chunk)
-            return carry
-
-        if len(places) == 1:
-            body(0, 0)
-        else:
-            lax.fori_loop(0, len(places), body, 0)
+                    unit(pl.multiple_of(groups[place] * GRP, GRP), GRP, chunk)
 
     groups = (y, up, down, far)
 
@@ -402,92 +398,92 @@
     s_ready("dt")
     s_z("dt")
     s_own("dt")
-    s_ready(2)
-    s_own(2)
     prepare(3)
     slot(2)
     across(2)
     s_next(0)
     s_near(1)
     across(1)
+    s_pair(1)
+    s_ready(2)
+    s_own(2)
+    s_z(2)
     slot(3)
     halo_wait(halo_b)
     halo_send(jnp.logical_and(halo_b, inner), head, at_up, at_down)
-    s_pair(1)
-    s_z(2)
     slot(4)
     prepare("b")
     s_near("dt")
     s_pair("dt")
-    s_ready(3)
-    s_own(3)
+    across(0)
     slot(5)
-    across(0)
     s_next(1)
     s_near(2)
-    s_far(0)
     slot(6)
     prepare("c")
     s_pair(2)
+    s_ready(3)
+    s_own(3)
     s_z(3)
+    slot(7)
+    s_next("dt")
+    s_far(0)
     halo_wait(jnp.logical_or(halo_c, halo_d))
     halo_send(jnp.logical_and(halo_c, inner), head, at_up)
     halo_send(jnp.logical_and(halo_d, inner), head, at_down)
+    slot(8)
+    s_next(2)
     s_ready("b")
     s_own("b")
-    slot(7)
-    s_next("dt")
     load_t.wait()
-    halo_wait(halo_rest)
+    halo_wait(halo_e)
     tok_wait(ZL)
     tok_wait(L0, L1, pieces=(3,))
     s_sib(0)
     units((0,), 0)
-    slot(8)
-    s_next(2)
     s_near(3)
-    s_pair(3)
     s_z("b")
     s_far(1)
+    s_pair(3)
+    slot(9)
+    tok_wait(L0, R0, L1, R1)
+    units((1,), 0)
     s_ready("c")
     s_own("c")
-    slot(9)
+    s_z("c")
+    s_far("dt")
+    s_near("b")
+    slot(10)
     s_sib(1)
-    units((0,), 1)
-    s_far("dt")
+    units((0, 1), 1)
+    s_far(2)
+    slot(11)
+    tok_wait(O0, O1, pieces=(3,))
+    halo_wait(halo_rest)
+    units((2,), 0, 1)
+    s_next(3)
+    s_pair("b")
+    s_near("c")
     s_sib("dt")
     unpack()
-    units((0,), "dt")
-    slot(10)
-    tok_wait(L0, R0, L1, R1)
-    units((1,), "dt", 0, 1)
-    slot(11)
-    tok_wait(O0, O1, pieces=(3,))
-    units((2,), 0)
-    s_next(3)
-    s_near("b")
-    s_pair("b")
-    s_z("c")
-    s_far(2)
+    units((0, 1, 2), "dt")
+    s_pair("c")
     s_sib(2)
     units((0, 1), 2)
     s_next("b")
-    s_near("c")
-    s_pair("c")
-    units((2,), "dt", 1, 2)
+    tok_far()
+    units((3,), "dt", 0)
+    s_next("c")
     s_far(3)
-    s_next("c")
+    units((2,), 2)
+    units((3,), 1, 2)
     s_far("b")
+    s_far("c")
     s_sib(3)
-    units((0, 1), 3)
-    s_far("c")
-    units((2,), 3)
-    tok_far()
-    units((3,), "dt", 0, 1)
-    units((3,), 2, 3)
+    units((0, 1, 2, 3), 3)
     s_sib("b")
+    s_sib("c")
     whole("b")
-    s_sib("c")
     whole("c")
 
     pltpu.make_async_copy(tok.at[pl.ds(0, 7 * TOK)], tok.at[pl.ds(0, 7 * TOK)], t_send).wait()

time: 126 us -> 121 us (0.960)
  Pallas kernels: 125 us -> 120 us
    pallas_call x1, Pallas kernels: 119 us -> 114 us  [on_device(): pl.pallas_call(kernel, out_shape=(pltpu.VMEM((ROWS, HPG * HEAD), bf16), p...]
where the time goes in v4:
time: 121 us
  Pallas kernels  120 us (99%)
    pallas_call x1, Pallas kernels, on_device(): pl.pallas_call(kernel, out_shape=(pltpu.VMEM((ROWS, HPG * HEAD), bf16), p...  114 us
    pallas_call x1, Pallas kernels, on_device(): pl.pallas_call(arrange, out_shape=(pltpu.VMEM((5, 8, KR, CW), bf16), pltp...  4.09 us

profile of v4, /device:TPU:0, one launch (start us, length us, event | category | flops | bytes accessed | tf_op | source)
XLA Modules:
  0.0 120.6 jit_solution(9473773545403388733)
XLA Ops:
  0.6 4.1 %shard_map.94 = (bf16[5,8,32,512]{3,2,1,0:T(8,128)(2,1)S(1)}, bf16[8,32,128]{2,1,0:T(8,128)(2,1)S(1)}) custom-call(s32[8]{0:T(128)} %group_order.1, s32[8,16]{1,0:T(8,128)} %head_order.1, bf16[32,20608]{1,0:T(8,128)(2,1)} %weight.1), custom_call_target="tpu_custom_call" | custom-call | flops 1048576 | bytes 3145728 | tf_op jit(solution)/shard_map/pallas_call | solution.py:531
  4.7 113.9 %shard_map.95 = (bf16[1024,1024]{1,0:T(8,128)(2,1)S(1)}, bf16[1024,512]{1,0:T(8,128)(2,1)S(1)}, f32[16,1024]{1,0:T(8,128)S(1)}) custom-call(bf16[128,4096]{1,0:T(8,128)(2,1)} %tokens.1, bf16[5,8,32,512]{3,2,1,0:T(8,128)(2,1)S(1)} %get-tuple-element.11.stage, bf16[8,32,128]{2,1,0:T(8,128)(2,1)S(1)} %get-tuple-element.12.stage_dt, f32[4,1024]{1,0:T(4,128)} %conv_x.1, ...), custom_call_target="tpu_custom_call" | custom-call | flops 21609054208 | bytes 6291456 | tf_op jit(solution)/shard_map/pallas_call | solution.py:540
  118.7 1.7 %shard_map.96 = (bf16[1024,1024]{1,0:T(8,128)(2,1)}, bf16[1024,512]{1,0:T(8,128)(2,1)}, f32[16,1024]{1,0:T(8,128)}) custom-call(bf16[1024,1024]{1,0:T(8,128)(2,1)S(1)} %get-tuple-element.13.gated_v, bf16[1024,512]{1,0:T(8,128)(2,1)S(1)} %get-tuple-element.14.states_v, f32[16,1024]{1,0:T(8,128)S(1)} %get-tuple-element.15.steps_v), custom_call_target="tpu_custom_call" | custom-call | bytes 3145728 | tf_op jit(solution)/shard_map/pallas_call | solution.py:565

commit v5 on v4

--- a/solution.py
+++ b/solution.py
@@ -24,7 +24,7 @@
 HALO = 16
 CW = 512
 ORDER = ("dt", 0, 1, 2, 3, "b", "c")
-BY_Z = (3, "b")
+BY_Z = ("b",)
 
 
 def arrange(group_order, head_order, weight, stage, stage_dt, held, lined, sems):
@@ -452,38 +452,38 @@
     s_own("c")
     s_z("c")
     s_far("dt")
-    s_near("b")
     slot(10)
     s_sib(1)
     units((0, 1), 1)
+    s_near("b")
     s_far(2)
     slot(11)
     tok_wait(O0, O1, pieces=(3,))
     halo_wait(halo_rest)
     units((2,), 0, 1)
     s_next(3)
-    s_pair("b")
-    s_near("c")
     s_sib("dt")
     unpack()
     units((0, 1, 2), "dt")
+    s_sib(2)
+    units((0, 1, 2), 2)
+    s_near("c")
+    s_pair("b")
     s_pair("c")
-    s_sib(2)
-    units((0, 1), 2)
+    s_far(3)
     s_next("b")
     tok_far()
-    units((3,), "dt", 0)
+    units((3,), "dt", 0, 1)
     s_next("c")
-    s_far(3)
-    units((2,), 2)
-    units((3,), 1, 2)
+    s_sib(3)
+    units((3,), 2)
+    units((0, 1), 3)
     s_far("b")
     s_far("c")
-    s_sib(3)
-    units((0, 1, 2, 3), 3)
+    units((2, 3), 3)
     s_sib("b")
+    whole("b")
     s_sib("c")
-    whole("b")
     whole("c")
 
     pltpu.make_async_copy(tok.at[pl.ds(0, 7 * TOK)], tok.at[pl.ds(0, 7 * TOK)], t_send).wait()

time: 121 us -> 120 us (level)
  no operation moved by 1% of the time
where the time goes in v5:
time: 120 us
  Pallas kernels  119 us (99%)
    pallas_call x1, Pallas kernels, on_device(): pl.pallas_call(kernel, out_shape=(pltpu.VMEM((ROWS, HPG * HEAD), bf16), p...  114 us
    pallas_call x1, Pallas kernels, on_device(): pl.pallas_call(arrange, out_shape=(pltpu.VMEM((5, 8, KR, CW), bf16), pltp...  4.09 us

profile of v5, /device:TPU:0, one launch (start us, length us, event | category | flops | bytes accessed | tf_op | source)
XLA Modules:
  0.0 120.2 jit_solution(9652510018818870032)
XLA Ops:
  0.6 4.1 %shard_map.94 = (bf16[5,8,32,512]{3,2,1,0:T(8,128)(2,1)S(1)}, bf16[8,32,128]{2,1,0:T(8,128)(2,1)S(1)}) custom-call(s32[8]{0:T(128)} %group_order.1, s32[8,16]{1,0:T(8,128)} %head_order.1, bf16[32,20608]{1,0:T(8,128)(2,1)} %weight.1), custom_call_target="tpu_custom_call" | custom-call | flops 1048576 | bytes 3145728 | tf_op jit(solution)/shard_map/pallas_call | solution.py:531
  4.7 113.5 %shard_map.95 = (bf16[1024,1024]{1,0:T(8,128)(2,1)S(1)}, bf16[1024,512]{1,0:T(8,128)(2,1)S(1)}, f32[16,1024]{1,0:T(8,128)S(1)}) custom-call(bf16[128,4096]{1,0:T(8,128)(2,1)} %tokens.1, bf16[5,8,32,512]{3,2,1,0:T(8,128)(2,1)S(1)} %get-tuple-element.11.stage, bf16[8,32,128]{2,1,0:T(8,128)(2,1)S(1)} %get-tuple-element.12.stage_dt, f32[4,1024]{1,0:T(4,128)} %conv_x.1, ...), custom_call_target="tpu_custom_call" | custom-call | flops 21609054208 | bytes 6291456 | tf_op jit(solution)/shard_map/pallas_call | solution.py:540
  118.3 1.7 %shard_map.96 = (bf16[1024,1024]{1,0:T(8,128)(2,1)}, bf16[1024,512]{1,0:T(8,128)(2,1)}, f32[16,1024]{1,0:T(8,128)}) custom-call(bf16[1024,1024]{1,0:T(8,128)(2,1)S(1)} %get-tuple-element.13.gated_v, bf16[1024,512]{1,0:T(8,128)(2,1)S(1)} %get-tuple-element.14.states_v, f32[16,1024]{1,0:T(8,128)S(1)} %get-tuple-element.15.steps_v), custom_call_target="tpu_custom_call" | custom-call | bytes 3145728 | tf_op jit(solution)/shard_map/pallas_call | solution.py:565

commit v6 on v5

--- a/solution.py
+++ b/solution.py
@@ -356,9 +356,9 @@
             value = silu(conv(conv_x[:, cols], size, 256)) * silu(proj[pl.ds(HALO, size), 0:256])
             gated[pl.ds(start, size), cols] = value.astype(jnp.bfloat16)
 
-    def whole(chunk):
-        for step in range(2):
-            unit(step * 2 * GRP, 2 * GRP, chunk)
+    def whole(chunk, steps=range(4)):
+        for step in steps:
+            unit(step * GRP, GRP, chunk)
 
     def unit_dt(group):
         start = pl.multiple_of(group * GRP, GRP)
@@ -477,10 +477,10 @@
     s_next("c")
     s_sib(3)
     units((3,), 2)
-    units((0, 1), 3)
+    whole(3, (0, 1))
     s_far("b")
     s_far("c")
-    units((2, 3), 3)
+    whole(3, (2, 3))
     s_sib("b")
     whole("b")
     s_sib("c")

time: 120 us -> 120 us (level)
  no operation moved by 1% of the time
where the time goes in v6:
time: 120 us
  Pallas kernels  119 us (99%)
    pallas_call x1, Pallas kernels, on_device(): pl.pallas_call(kernel, out_shape=(pltpu.VMEM((ROWS, HPG * HEAD), bf16), p...  113 us
    pallas_call x1, Pallas kernels, on_device(): pl.pallas_call(arrange, out_shape=(pltpu.VMEM((5, 8, KR, CW), bf16), pltp...  4.09 us

profile of v6, /device:TPU:0, one launch (start us, length us, event | category | flops | bytes accessed | tf_op | source)
XLA Modules:
  0.0 119.7 jit_solution(18037669692875638418)
XLA Ops:
  0.6 4.1 %shard_map.94 = (bf16[5,8,32,512]{3,2,1,0:T(8,128)(2,1)S(1)}, bf16[8,32,128]{2,1,0:T(8,128)(2,1)S(1)}) custom-call(s32[8]{0:T(128)} %group_order.1, s32[8,16]{1,0:T(8,128)} %head_order.1, bf16[32,20608]{1,0:T(8,128)(2,1)} %weight.1), custom_call_target="tpu_custom_call" | custom-call | flops 1048576 | bytes 3145728 | tf_op jit(solution)/shard_map/pallas_call | solution.py:531
  4.7 113.0 %shard_map.95 = (bf16[1024,1024]{1,0:T(8,128)(2,1)S(1)}, bf16[1024,512]{1,0:T(8,128)(2,1)S(1)}, f32[16,1024]{1,0:T(8,128)S(1)}) custom-call(bf16[128,4096]{1,0:T(8,128)(2,1)} %tokens.1, bf16[5,8,32,512]{3,2,1,0:T(8,128)(2,1)S(1)} %get-tuple-element.11.stage, bf16[8,32,128]{2,1,0:T(8,128)(2,1)S(1)} %get-tuple-element.12.stage_dt, f32[4,1024]{1,0:T(4,128)} %conv_x.1, ...), custom_call_target="tpu_custom_call" | custom-call | flops 21609054208 | bytes 6291456 | tf_op jit(solution)/shard_map/pallas_call | solution.py:540
  117.8 1.7 %shard_map.96 = (bf16[1024,1024]{1,0:T(8,128)(2,1)}, bf16[1024,512]{1,0:T(8,128)(2,1)}, f32[16,1024]{1,0:T(8,128)}) custom-call(bf16[1024,1024]{1,0:T(8,128)(2,1)S(1)} %get-tuple-element.13.gated_v, bf16[1024,512]{1,0:T(8,128)(2,1)S(1)} %get-tuple-element.14.states_v, f32[16,1024]{1,0:T(8,128)S(1)} %get-tuple-element.15.steps_v), custom_call_target="tpu_custom_call" | custom-call | bytes 3145728 | tf_op jit(solution)/shard_map/pallas_call | solution.py:565
